TPU v7x, 512 devices: a whole 4x8x8 slice. The times are simulated.
512 devices in a mesh: scen: 32 (over x, z), area: 16 (over y, core).
Axes of the slice: x: 4, y: 8, z: 8, core: 2. Of those that a mesh axis runs over, the one named last changes fastest.
Arguments:
- cost_lin: float32 [1536, 16, 7, 384], P('scen', 'area'), may hold values from -6 to 6
- na_dual: float32 [1536, 16, 7, 384], P('scen', 'area'), may hold values from -6 to 6
- prior_mean: float32 [1536, 16, 7, 384], P('scen', 'area'), may hold values from -6 to 6
- kkt_inverse: bfloat16 [16, 7, 384, 384], P('area'), may hold values from -0.3125 to 0.3125
- tie_coef: float32 [16, 16], P('area'), may hold values from 0.3 to 1.5
- res_count: int32 [16], P('area'), may hold values from 4 to 16, as said below
- line_class: int32 [16, 2], P('area'), may hold values from 1 to 3, as said below
- node_of: int32 [7, 1536], P(None, 'scen'), may hold values from 0 to 63, as said below
Outputs:
- node_mean: float32 [1536, 16, 7, 384], P('scen', 'area')
- new_dual: float32 [1536, 16, 7, 384], P('scen', 'area')
Inputs may be any that keep to these rules, and one draw needn't show every extreme that they name: `res_count`: some area has 16 reservoirs and some area has 4. line_class[a, 0] equals line_class[a-1, 1], area indices taken modulo 16. `node_of`: at section c the nodes are 0 to 2**c - 1, every one of them holds at least one scenario, and scenarios that share a node at section c + 1 share it at section c.
All inputs are finite; a program needn't handle non-finite values.
Results may differ from a plain program's by a relative error of at most 0.004.
Values sent between devices are 32-bit elements; how exact they have to be, the bound alone decides.
A program may use at most 64 MiB of HBM per device.

v0:
```python
import jax
import jax.numpy as jnp
from jax import lax
from jax.sharding import PartitionSpec as P

SWEEPS = 2


RHO = 1.0
RHO_TIE = 0.5


def extended(block, sides, width):
    for axis, dim in sides:
        count = lax.axis_size(axis)
        forward = [(i, i + 1) for i in range(count - 1)]
        forward.append((count - 1, 0))
        backward = [(target, source) for source, target in forward]
        low = lax.ppermute(
            lax.slice_in_dim(block, block.shape[dim] - width, None, axis=dim), axis, forward
        )
        high = lax.ppermute(lax.slice_in_dim(block, 0, width, axis=dim), axis, backward)
        block = jnp.concatenate([low, block, high], axis=dim)
    return block


def on_device(cost_lin, na_dual, prior_mean, kkt_inverse, tie_coef, res_count, line_class, node_of):
    scen_local = cost_lin.shape[0]
    span_count = cost_lin.shape[2]
    row_width = cost_lin.shape[3]
    slot_count = tie_coef.shape[1]
    hour_count = row_width // slot_count
    slot_ids = lax.broadcasted_iota(jnp.int32, (slot_count,), 0)
    live_slots = (slot_ids < res_count[0]).astype(jnp.float32)
    export_weight = tie_coef[0] * live_slots
    mask_full = jnp.tile(live_slots, hour_count)
    left_weight = line_class[0, 0].astype(jnp.float32) / 3.0
    right_weight = line_class[0, 1].astype(jnp.float32) / 3.0
    anchor = RHO * prior_mean[:, 0] - cost_lin[:, 0] - na_dual[:, 0]
    inverse_blocks = kkt_inverse[0]
    current = prior_mean[:, 0]
    for sweep_index in range(SWEEPS):
        blocks = current.reshape(scen_local, span_count, hour_count, slot_count)
        export = jnp.sum(blocks * export_weight, axis=3).reshape(
            scen_local, 1, span_count * hour_count
        )
        flanked = extended(export, (("area", 1),), 1)
        own_export = flanked[:, 1]
        tie_gap = right_weight * (flanked[:, 2] - own_export) + left_weight * (
            flanked[:, 0] - own_export
        )
        coupling = tie_gap.reshape(scen_local, span_count, hour_count, 1) * export_weight
        target = anchor + RHO_TIE * coupling.reshape(scen_local, span_count, row_width)
        target_low = target.astype(jnp.bfloat16)
        solved = jnp.einsum(
            "sck,cjk->scj", target_low, inverse_blocks, preferred_element_type=jnp.float32
        )
        current = solved * mask_full
    indicators = []
    partials = []
    member_counts = []
    for section_index in range(span_count):
        group_count = 2**section_index
        indicator = (
            node_of[section_index][:, None] == lax.broadcasted_iota(jnp.int32, (1, group_count), 1)
        ).astype(jnp.float32)
        indicators.append(indicator)
        partials.append(
            lax.dot_general(
                indicator,
                current[:, section_index],
                (((0,), (0,)), ((), ())),
                precision=lax.Precision.HIGHEST,
                preferred_element_type=jnp.float32,
            )
        )
        member_counts.append(jnp.sum(indicator, axis=0))
    local_sums = jnp.concatenate(partials, axis=0)
    local_sizes = jnp.concatenate(member_counts, axis=0)
    total_sums, group_sizes = lax.psum((local_sums, local_sizes), "scen")
    group_means = total_sums / group_sizes[:, None]
    expanded = []
    offset = 0
    for section_index in range(span_count):
        group_count = 2**section_index
        expanded.append(
            jnp.dot(
                indicators[section_index],
                group_means[offset : offset + group_count],
                precision=lax.Precision.HIGHEST,
                preferred_element_type=jnp.float32,
            )
        )
        offset = offset + group_count
    node_mean = jnp.stack(expanded, axis=1)
    new_dual = na_dual[:, 0] + RHO * (current - node_mean)
    return (node_mean[:, None], new_dual[:, None])


def solution(mesh):
    placed = (
        P("scen", "area", None, None),
        P("scen", "area", None, None),
        P("scen", "area", None, None),
        P("area", None, None, None),
        P("area", None),
        P("area"),
        P("area", None),
        P(None, "scen"),
    )
    return jax.shard_map(
        on_device,
        mesh=mesh,
        in_specs=placed,
        out_specs=(P("scen", "area", None, None), P("scen", "area", None, None)),
        check_vma=False,
    )
```

profile of v0, /device:TPU:8, one launch (start us, length us, event | category | flops | bytes accessed | tf_op | source)
XLA Modules:
  0.0 281.1 jit_solution(14529994823974223650)
XLA Ops:
  8.0 1.7 copy.28
  10.2 1.7 collective-permute-start
  11.9 0.6 slice_bitcast_fusion.14
  12.5 0.7 convert_reduce_fusion.6
  13.2 0.6 fusion.55
  13.8 0.6 convert_reduce_fusion
  14.4 0.7 convert_reduce_fusion.1
  15.1 0.6 convert_reduce_fusion.2
  15.7 0.6 convert_reduce_fusion.3
  16.3 0.7 convert_reduce_fusion.4
  18.7 1.2 copy.29
  19.9 3.1 %fusion.7 = f32[48,7,384]{2,0,1:T(8,128)} fusion(bf16[1,7,384,384]{3,2,1,0:T(8,128)(2,1)S(1)} %copy-done, f32[48,7,384]{2,0,1:T(8,128)} %copy.29, f32[384]{0:T(512)S(1)} %mul.133, f32[384]{0:T(512)S(1)} %mul.129, f32[48,1,7,384]{3,1,2,0:T(1,128)} %param.8, f32[48,1,7,384]{3,1,2,0:T(1,128)} %param.10, f32[48,1,7,384]{3,1,2,0:T(1,128)} %param.9), kind=kOutput, calls=%fused_computation.7 | convolution fusion | flops 99993600 | bytes 4647936 | tf_op jit(solution)/shard_map/sck,cjk->scj/dot_general | solution.py:55
  23.0 1.5 copy.30
  24.5 1.0 multiply_reduce_fusion
  25.4 4.2 %collective-permute-start.2 = (f32[48,1,168]{0,2,1:T(8,128)S(1)}, f32[48,1,168]{0,2,1:T(8,128)S(1)}, u32[]{:S(2)}, u32[]{:S(2)}) collective-permute-start(f32[48,1,168]{0,2,1:T(8,128)S(1)} %bitcast.128), channel_id=1, source_target_pairs={{1,0},{2,1},{3,2},{4,3},{5,4},{6,5},{7,6},{8,7},{9,8},{10,9},{11,1... | collective-permute-start | bytes 96776 | tf_op jit(solution)/shard_map/ppermute | solution.py:22
  29.8 1.4 concatenate.7
  31.2 77.6 %psum.15 = f32[127]{0:T(128)} all-reduce(f32[127]{0:T(128)S(1)} %concatenate.7), channel_id=1, replica_groups=mesh['scen'=32,'area'=16] {'scen'}, use_global_device_ids=true, to_apply=%region_10.0 | all-reduce | flops 127 | bytes 1016 | tf_op jit(solution)/shard_map/psum | solution.py:80
  109.0 1.2 copy.31
  110.2 2.3 fusion.13
  113.8 6.2 %concatenate.6 = f32[127,384]{1,0:T(8,128)} concatenate(f32[1,384]{1,0:T(1,128)S(1)} %fusion.34, f32[2,384]{1,0:T(2,128)S(1)} %fusion.33, f32[4,384]{1,0:T(4,128)S(1)} %fusion.32, f32[8,384]{1,0:T(8,128)S(1)} %fusion.31, f32[16,384]{1,0:T(8,128)S(1)} %fusion.30, f32[32,384]{1,0:T(8,128)S(1)} %fusion.29, f32[64,384]{1,0:T(8,128)S(1)} %fusion.28), dimensions={0} | concatenate | bytes 390144 | tf_op jit(solution)/shard_map/concatenate | solution.py:78
  120.0 148.9 %all-reduce.2.cloned.1.call-done = f32[127,384]{1,0:T(8,128)} async-done(((f32[127,384]{1,0:T(8,128)}), f32[127,384]{1,0:T(8,128)}) %all-reduce.2.cloned.1.call-update) | async-done | bytes 195088 | tf_op jit(solution)/shard_map/psum | solution.py:80
  268.9 1.0 broadcast_divide_fusion
  271.6 1.3 copy.33
  272.9 1.3 copy.32
  (59 shorter events, 3.8 us)
Async XLA Ops:
  7.2 12.7 %copy-start = (bf16[1,7,384,384]{3,2,1,0:T(8,128)(2,1)S(1)}, bf16[1,7,384,384]{3,2,1,0:T(8,128)(2,1)}, u32[]{:S(2)}) copy-start(bf16[1,7,384,384]{3,2,1,0:T(8,128)(2,1)} %param.11) | copy-start | bytes 6193156
  7.2 2.6 copy-start.10
  7.2 261.7 %all-reduce.2.cloned.1.call-start = ((), (), s32[]{:S(2)}) async-start(), calls=%async_computation | async-start | bytes 393216 | tf_op jit(solution)/shard_map/psum | solution.py:80
  8.0 3.9 %copy-start.2 = (s32[7,48]{1,0:T(8,128)S(1)}, s32[7,48]{1,0:T(8,128)}, u32[]{:S(2)}) copy-start(s32[7,48]{1,0:T(8,128)} %param.15) | copy-start | bytes 4036
  9.8 3.4 %copy-start.8 = (s32[1,2]{1,0:T(1,128)S(1)}, s32[1,2]{1,0:T(1,128)}, u32[]{:S(2)}) copy-start(s32[1,2]{1,0:T(1,128)} %param.14) | copy-start | bytes 28
  9.8 8.5 %copy-start.5 = (f32[16]{0:T(128)}, f32[16]{0:T(128)S(1)}, u32[]{:S(2)}) copy-start(f32[16]{0:T(128)S(1)} %compare_select_fusion) | copy-start | bytes 196
  10.2 8.4 %collective-permute-start.1 = (f32[48,1,168]{0,2,1:T(8,128)S(1)}, f32[48,1,168]{0,2,1:T(8,128)S(1)}, u32[]{:S(2)}, u32[]{:S(2)}) collective-permute-start(f32[48,1,168]{0,2,1:T(8,128)S(1)} %bitcast.126), channel_id=1, source_target_pairs={{0,1},{1,2},{2,3},{3,4},{4,5},{5,6},{6,7},{7,8},{8,9},{9,10},{10,1... | collective-permute-start | bytes 96776 | tf_op jit(solution)/shard_map/ppermute | solution.py:19
  10.2 8.3 %collective-permute-start = (f32[48,1,168]{0,2,1:T(8,128)S(1)}, f32[48,1,168]{0,2,1:T(8,128)S(1)}, u32[]{:S(2)}, u32[]{:S(2)}) collective-permute-start(f32[48,1,168]{0,2,1:T(8,128)S(1)} %bitcast.127), channel_id=1, source_target_pairs={{1,0},{2,1},{3,2},{4,3},{5,4},{6,5},{7,6},{8,7},{9,8},{10,9},{11,1... | collective-permute-start | bytes 96776 | tf_op jit(solution)/shard_map/ppermute | solution.py:22
  12.5 5.9 %copy-start.6 = (s32[48]{0:T(128)}, s32[48]{0:T(128)S(1)}, u32[]{:S(2)}) copy-start(s32[48]{0:T(128)S(1)} %get-tuple-element.8) | copy-start | bytes 580
  24.4 5.2 %copy-start.3 = (s32[48]{0:T(128)S(1)}, s32[48]{0:T(128)}, u32[]{:S(2)}) copy-start(s32[48]{0:T(128)} %get-tuple-element.12) | copy-start | bytes 580
  25.4 83.4 %collective-permute-start.2 = (f32[48,1,168]{0,2,1:T(8,128)S(1)}, f32[48,1,168]{0,2,1:T(8,128)S(1)}, u32[]{:S(2)}, u32[]{:S(2)}) collective-permute-start(f32[48,1,168]{0,2,1:T(8,128)S(1)} %bitcast.128), channel_id=1, source_target_pairs={{1,0},{2,1},{3,2},{4,3},{5,4},{6,5},{7,6},{8,7},{9,8},{10,9},{11,1... | collective-permute-start | bytes 96776 | tf_op jit(solution)/shard_map/ppermute | solution.py:22
  29.7 79.2 %collective-permute-start.3 = (f32[48,1,168]{0,2,1:T(8,128)S(1)}, f32[48,1,168]{0,2,1:T(8,128)S(1)}, u32[]{:S(2)}, u32[]{:S(2)}) collective-permute-start(f32[48,1,168]{0,2,1:T(8,128)S(1)} %bitcast.129), channel_id=1, source_target_pairs={{0,1},{1,2},{2,3},{3,4},{4,5},{5,6},{6,7},{7,8},{8,9},{9,10},{10,1... | collective-permute-start | bytes 96776 | tf_op jit(solution)/shard_map/ppermute | solution.py:19
  110.2 2.3 copy-start.7
  110.2 3.3 %copy-start.4 = (s32[48]{0:T(128)S(1)}, s32[48]{0:T(128)}, u32[]{:S(2)}) copy-start(s32[48]{0:T(128)} %get-tuple-element.12) | copy-start | bytes 580
  110.2 158.8 %copy-start.9 = (f32[127]{0:T(128)S(1)}, f32[127]{0:T(128)}, u32[]{:S(2)}) copy-start(f32[127]{0:T(128)} %psum.15) | copy-start | bytes 1528
  112.5 159.0 %copy-start.1 = (f32[48,1,7,384]{3,1,2,0:T(1,128)S(1)}, f32[48,1,7,384]{3,1,2,0:T(1,128)}, u32[]{:S(2)}) copy-start(f32[48,1,7,384]{3,1,2,0:T(1,128)} %param.9) | copy-start | bytes 1548292
Sparse Core Ops, SparseCore 0:
  120.1 148.7 all-reduce.1
where the time goes:
time: 282 us; the launch traced here: 281 us
  waiting for transfers between devices  149 us (53%)
  blocking collectives  77.6 us (28%)
  local copies, waits for them, and re-layouts  17.5 us (6%)
  between operations  16.4 us (6%)
  matrix products  8.02 us (3%)
  other arithmetic  6.54 us (2%)
  starting transfers between devices  6.02 us (2%)
    psum x1, waiting for transfers between devices, on_device(): total_sums, group_sizes = lax.psum((local_sums, local_sizes), 'scen')  149 us
    psum x1, blocking collectives, on_device(): total_sums, group_sizes = lax.psum((local_sums, local_sizes), 'scen')  77.6 us
    concatenate x1, local copies, waits for them, and re-layouts, on_device(): local_sums = jnp.concatenate(partials, axis=0)  6.23 us
    ppermute x2, starting transfers between devices, extended(): lax.ppermute(lax.slice_in_dim(block, 0, width, axis=dim), axis, backward)  5.96 us
  transfers between devices with their start and end apart: 5, of which 1 were waited for; matrix products, arithmetic and copies ran while one was open for 2% of the time, Pallas kernels for 0%

commit v1 on v0

v1 whole, which is shorter than its diff:
```python
import functools

import jax
import jax.numpy as jnp
from jax import lax
from jax.experimental import pallas as pl
from jax.experimental.pallas import tpu as pltpu
from jax.sharding import PartitionSpec as P

F32 = jnp.float32
BF16 = jnp.bfloat16
MESH = pl.DeviceIdType.MESH

SCEN_L = 48
SPANS = 7
K = 384
RES = 16
BLK = 128
NB = K // BLK
ROWS = SCEN_L * SPANS
STRIDE = SPANS * NB
NX, NZ, NA = 4, 8, 16
NODES = 128
CHUNK = NODES // NZ
WIDE = K + BLK

BASE = (126, 124, 120, 112, 96, 64, 0)
SLOT = (0, 1, 2, 4, 5, 6, 3)

X_OFFS = ((2, 0), (1, 0), (3, 0))
Z_OFFS = tuple((0, d) for d in (4, 3, 5, 2, 6, 1, 7))


def split(value):
    high = value.astype(BF16)
    low = (value - high.astype(F32)).astype(BF16)
    return high, low


def dot(a, b):
    return jnp.dot(a, b, preferred_element_type=F32)


def dot_nt(a, b):
    return lax.dot_general(a, b, (((1,), (1,)), ((), ())), preferred_element_type=F32)


def kernel(
    cost_h, dual_h, prior_h, kkt_h, tie_h, count_h, line_h, node_h,
    mean_o, newdual_o,
    cost_v, dual_v, prior_v, kkt_v, tie_r, count_r, line_r, node_r, tie_v, node_v, sel_v, spread_v, spread_all_v, pick_v, pickt_v,
    anchor_v, base_v, kgap_v,
    exp_v, low_v, high_v,
    part_v, rz_v, sumz_v, rx_v, total_v, gather_v,
    gsum_v, gx_v, gsumx_v, gz_v,
    in_sem, es_sem, er_sem, zs_sem, zr_sem, xs_sem, xr_sem, as_sem, ar_sem,
    gxs_sem, gxr_sem, gzs_sem, gzr_sem,
):
    me = lax.axis_index("scen")
    area = lax.axis_index("area")
    my_x = me // NZ
    my_z = lax.rem(me, NZ)
    up = lax.rem(area + 1, NA)
    down = lax.rem(area + NA - 1, NA)

    def peer_z(off):
        return lax.rem(my_z + off[1], NZ)

    def peer(off):
        return lax.rem(my_x + off[0], NX) * NZ + peer_z(off)

    def send(src, dst, send_sem, recv_sem, device):
        pltpu.make_async_remote_copy(
            src_ref=src, dst_ref=dst, send_sem=send_sem, recv_sem=recv_sem,
            device_id=device, device_id_type=MESH,
        ).start()

    def wait(ref, sem):
        pltpu.make_async_copy(ref, ref, sem).wait()

    loads = [
        pltpu.make_async_copy(src, dst, in_sem.at[i])
        for i, (src, dst) in enumerate(
            (
                (prior_h, prior_v), (cost_h, cost_v), (dual_h, dual_v), (kkt_h, kkt_v),
                (tie_h, tie_r), (count_h, count_r), (line_h, line_r), (node_h, node_r),
            )
        )
    ]
    for i in (4, 5, 6, 7, 0, 1, 2, 3):
        loads[i].start()

    barrier = pltpu.get_barrier_semaphore()
    for off in Z_OFFS + X_OFFS:
        pl.semaphore_signal(barrier, inc=1, device_id={"scen": peer(off)}, device_id_type=MESH)
    for neighbour in (up, down):
        pl.semaphore_signal(barrier, inc=1, device_id={"area": neighbour}, device_id_type=MESH)

    rows = lax.broadcasted_iota(jnp.int32, (K, BLK), 0)
    lanes = lax.broadcasted_iota(jnp.int32, (K, BLK), 1)
    rows_w = lax.broadcasted_iota(jnp.int32, (BLK, K), 0)
    lanes_w = lax.broadcasted_iota(jnp.int32, (BLK, K), 1)
    for j in range(4):
        sel_v[j] = jnp.where(lanes == 32 * j + (rows >> 4), 1.0, 0.0).astype(BF16)
        spread_v[j] = jnp.where(rows_w == 32 * j + (lanes_w >> 4), 1.0, 0.0).astype(BF16)
    spread_all_v[...] = jnp.where((rows_w & 31) == (lanes_w >> 4), 1.0, 0.0).astype(BF16)

    for i in (4, 5, 6, 7):
        loads[i].wait()
    tie_v[...] = jnp.zeros((8, BLK), F32)
    tie_v[0:1, 0:RES] = tie_r[...]
    tie = tie_v[...]
    for shift in (16, 32, 64):
        tie = tie + pltpu.roll(tie, shift, 1)
    lane_row = lax.broadcasted_iota(jnp.int32, (1, BLK), 1)
    live = jnp.where((lane_row & 15) < count_r[0], 1.0, 0.0)
    weight = tie[0:1] * live
    live3 = jnp.concatenate([live] * NB, axis=1)
    weight3 = jnp.concatenate([weight] * NB, axis=1)
    left_weight = jnp.full((1, BLK), line_r[0, 0], jnp.int32).astype(F32) / 3.0
    right_weight = jnp.full((1, BLK), line_r[0, 1], jnp.int32).astype(F32) / 3.0

    node_v[...] = jnp.full((BLK, BLK), -1.0, F32)
    node_v[0:SPANS, 0:SCEN_L] = node_r[...].astype(F32)
    node_t = jnp.transpose(node_v[...])
    node_lane = lax.broadcasted_iota(jnp.int32, (SCEN_L, BLK), 1).astype(F32)
    picks = []
    for c in range(SPANS):
        picks.append(jnp.where(node_lane - BASE[c] == node_t[0:SCEN_L, c : c + 1], 1.0, 0.0))
    picks.append(jnp.zeros((K - ROWS, BLK), F32))
    pick = jnp.concatenate(picks, axis=0)
    pickt_v[...] = jnp.transpose(pick).astype(BF16)
    pick_b = pick[0:ROWS].astype(BF16)
    pick_v[:, 0:BLK] = pick_b
    pick_v[:, BLK:] = pick_b

    def block(ref, c):
        return jnp.concatenate(
            [ref[pl.ds(c * NB + b, SCEN_L, stride=STRIDE), :] for b in range(NB)], axis=1
        )

    def exports(value_of, sweep):
        groups = [None, None]
        for c in range(SPANS):
            g, j = SLOT[c] // 4, SLOT[c] % 4
            high, low = split(value_of(c) * weight3)
            part = dot(jnp.concatenate([high, low], axis=0), sel_v[j])
            part = part[0:SCEN_L] + part[SCEN_L:]
            groups[g] = part if groups[g] is None else groups[g] + part
        exp_v[sweep] = jnp.concatenate(groups, axis=0)

    def send_exports(sweep):
        send(exp_v.at[sweep], low_v.at[sweep], es_sem.at[sweep, 0], er_sem.at[sweep, 0], {"area": up})
        send(exp_v.at[sweep], high_v.at[sweep], es_sem.at[sweep, 1], er_sem.at[sweep, 1], {"area": down})

    def tie_gap(sweep):
        wait(low_v.at[sweep], er_sem.at[sweep, 0])
        wait(high_v.at[sweep], er_sem.at[sweep, 1])
        own = exp_v[sweep]
        return right_weight * (high_v[sweep] - own) + left_weight * (low_v[sweep] - own)

    def targets(gap):
        high, low = split(gap)
        found = []
        for c in range(SPANS):
            g, j = SLOT[c] // 4, SLOT[c] % 4
            rows_g = slice(g * SCEN_L, (g + 1) * SCEN_L)
            wide = dot(jnp.concatenate([high[rows_g], low[rows_g]], axis=0), spread_v[j])
            coupling = 0.5 * weight3 * (wide[0:SCEN_L] + wide[SCEN_L:])
            found.append((anchor_v[c * SCEN_L : (c + 1) * SCEN_L, :] + coupling).astype(BF16))
        return found

    loads[0].wait()
    exports(lambda c: block(prior_v, c), 0)

    loads[1].wait()
    loads[2].wait()
    for c in range(SPANS):
        anchor_v[c * SCEN_L : (c + 1) * SCEN_L, :] = (
            block(prior_v, c) - block(cost_v, c) - block(dual_v, c)
        )
    loads[3].wait()
    highs, lows = [], []
    for c in range(SPANS):
        high, low = split(anchor_v[c * SCEN_L : (c + 1) * SCEN_L, :])
        both = dot_nt(jnp.concatenate([high, low], axis=0), kkt_v[c])
        high, low = split(both[0:SCEN_L] + both[SCEN_L:])
        highs.append(high)
        lows.append(low)
    pick_t = pickt_v[:, 0:ROWS]
    part = dot(pick_t, jnp.concatenate(highs, axis=0)) + dot(pick_t, jnp.concatenate(lows, axis=0))
    sizes = dot(pick_t, jnp.ones((ROWS, BLK), BF16))
    for i in range(NZ):
        rows_i = slice(i * CHUNK, (i + 1) * CHUNK)
        part_v[i, :, 0:K] = part[rows_i]
        part_v[i, :, K:] = sizes[rows_i]

    pl.semaphore_wait(barrier, len(Z_OFFS) + len(X_OFFS) + 2)
    send_exports(0)
    for n, off in enumerate(Z_OFFS):
        send(part_v.at[peer_z(off)], rz_v.at[n], zs_sem, zr_sem, {"scen": peer(off)})

    first = targets(tie_gap(0))
    exports(lambda c: dot_nt(first[c], kkt_v[c]), 1)
    send_exports(1)

    gap = tie_gap(1)
    gap_high, gap_low = split(gap)
    stacked = []
    for half in (gap_high, gap_low):
        stacked.append(
            jnp.concatenate(
                [half[SLOT[c] // 4 * SCEN_L : (SLOT[c] // 4 + 1) * SCEN_L] for c in range(SPANS)],
                axis=0,
            )
        )
    gap_part = dot(pick_t, stacked[0]) + dot(pick_t, stacked[1])
    node_row = lax.broadcasted_iota(jnp.int32, (NODES // 2, BLK), 0) + NODES // 2
    group = lax.broadcasted_iota(jnp.int32, (NODES // 2, BLK), 1) >> 5
    place = jnp.zeros((NODES // 2, BLK), jnp.int32) + SLOT[5] % 4
    for c in (4, 3, 2, 1, 0):
        place = jnp.where(node_row >= BASE[c], SLOT[c] % 4, place)
    upper = group == SLOT[6] % 4
    lower = group == place
    gsum_v[...] = jnp.where(upper, gap_part[0 : NODES // 2], 0.0) + jnp.where(
        lower, gap_part[NODES // 2 :], 0.0
    )
    for n, off in enumerate(X_OFFS):
        send(gsum_v, gx_v.at[n], gxs_sem, gxr_sem, {"scen": peer(off)})

    wait(rz_v, zr_sem)
    acc = part_v[my_z]
    for n in range(len(Z_OFFS)):
        acc = acc + rz_v[n]
    sumz_v[...] = acc
    for n, off in enumerate(X_OFFS):
        send(sumz_v, rx_v.at[n], xs_sem, xr_sem, {"scen": peer(off)})

    second = targets(gap)
    for c in range(SPANS):
        current = dot_nt(second[c], kkt_v[c]) * live3
        base_v[c * SCEN_L : (c + 1) * SCEN_L, :] = block(dual_v, c) + current

    wait(gx_v, gxr_sem)
    gacc = gsum_v[...]
    for n in range(len(X_OFFS)):
        gacc = gacc + gx_v[n]
    gsumx_v[...] = gacc
    for n, off in enumerate(Z_OFFS):
        send(gsumx_v, gz_v.at[n], gzs_sem, gzr_sem, {"scen": peer(off)})

    wait(rx_v, xr_sem)
    acc = sumz_v[...]
    for n in range(len(X_OFFS)):
        acc = acc + rx_v[n]
    total_v[...] = acc
    for n, off in enumerate(Z_OFFS):
        send(total_v, gather_v.at[my_z], as_sem, ar_sem.at[n], {"scen": peer(off)})
    gather_v[my_z] = acc

    wait(gz_v, gzr_sem)
    gacc = gsumx_v[...]
    for n in range(len(Z_OFFS)):
        gacc = gacc + gz_v[n]
    summed = jnp.concatenate([jnp.where(upper, gacc, 0.0), jnp.where(lower, gacc, 0.0)], axis=0)
    high, low = split(summed)
    wide = dot(jnp.concatenate([high, low], axis=0), spread_all_v[...])
    coupling = 0.5 * weight3 * (wide[0:NODES] + wide[NODES:])
    high, low = split(coupling)
    for c, first_row, count in ((6, 0, 64), (5, 64, 32), (4, 96, 16)):
        rows_c = slice(first_row, first_row + count)
        both = dot_nt(jnp.concatenate([high[rows_c], low[rows_c]], axis=0), kkt_v[c])
        kgap_v[rows_c, :] = both[0:count] + both[count:]
    small = jnp.concatenate([high[112:128], low[112:128]], axis=0)
    row_s = lax.broadcasted_iota(jnp.int32, (CHUNK, K), 0) + 112
    rest = jnp.zeros((CHUNK, K), F32)
    for c in (3, 2, 1, 0):
        both = dot_nt(small, kkt_v[c])
        inside = (row_s >= BASE[c]) & (row_s < BASE[c] + 2**c)
        rest = rest + jnp.where(inside, both[0:CHUNK] + both[CHUNK:], 0.0)
    kgap_v[112:128, :] = rest

    for n, off in enumerate(Z_OFFS):
        source = lax.rem(my_z + NZ - off[1], NZ)
        wait(gather_v.at[source], ar_sem.at[n])
    highs, lows = [], []
    for i in range(NZ):
        sizes_i = jnp.maximum(gather_v[i, :, K:], 1.0)
        scale = jnp.concatenate([1.0 / sizes_i] * NB, axis=1)
        average = (gather_v[i, :, 0:K] + kgap_v[i * CHUNK : (i + 1) * CHUNK, :]) * scale * live3
        high, low = split(average)
        highs.append(high)
        lows.append(low)
    averages = jnp.concatenate(highs + lows, axis=0)
    for c in range(SPANS):
        rows_c = slice(c * SCEN_L, (c + 1) * SCEN_L)
        node_mean = dot(pick_v[rows_c, :], averages)
        new_dual = base_v[rows_c, :] - node_mean
        for b in range(NB):
            place_b = pl.ds(c * NB + b, SCEN_L, stride=STRIDE)
            mean_o[place_b, :] = node_mean[:, b * BLK : (b + 1) * BLK]
            newdual_o[place_b, :] = new_dual[:, b * BLK : (b + 1) * BLK]

    for sweep in range(2):
        wait(exp_v.at[sweep], es_sem.at[sweep, 0])
        wait(exp_v.at[sweep], es_sem.at[sweep, 1])
    wait(rz_v, zs_sem)
    wait(rx_v, xs_sem)
    wait(rz_v, as_sem)
    wait(gx_v, gxs_sem)
    wait(gz_v, gzs_sem)


def on_device(cost_lin, na_dual, prior_mean, kkt_inverse, tie_coef, res_count, line_class, node_of):
    flat = (SCEN_L * STRIDE, BLK)
    any_spec = pl.BlockSpec(memory_space=pl.ANY)
    vmem = pl.BlockSpec(memory_space=pltpu.VMEM)
    dma = pltpu.SemaphoreType.DMA
    nz, nx = NZ - 1, NX - 1
    scratch = [
        pltpu.VMEM(flat, F32),
        pltpu.VMEM(flat, F32),
        pltpu.VMEM(flat, F32),
        pltpu.VMEM((SPANS, K, K), BF16),
        pltpu.VMEM((1, RES), F32),
        pltpu.SMEM((1,), jnp.int32),
        pltpu.SMEM((1, 2), jnp.int32),
        pltpu.VMEM((SPANS, SCEN_L), jnp.int32),
        pltpu.VMEM((8, BLK), F32),
        pltpu.VMEM((BLK, BLK), F32),
        pltpu.VMEM((4, K, BLK), BF16),
        pltpu.VMEM((4, BLK, K), BF16),
        pltpu.VMEM((BLK, K), BF16),
        pltpu.VMEM((ROWS, 2 * BLK), BF16),
        pltpu.VMEM((BLK, K), BF16),
        pltpu.VMEM((ROWS, K), F32),
        pltpu.VMEM((ROWS, K), F32),
        pltpu.VMEM((NODES, K), F32),
        pltpu.VMEM((2, 2 * SCEN_L, BLK), F32),
        pltpu.VMEM((2, 2 * SCEN_L, BLK), F32),
        pltpu.VMEM((2, 2 * SCEN_L, BLK), F32),
        pltpu.VMEM((NZ, CHUNK, WIDE), F32),
        pltpu.VMEM((nz, CHUNK, WIDE), F32),
        pltpu.VMEM((CHUNK, WIDE), F32),
        pltpu.VMEM((nx, CHUNK, WIDE), F32),
        pltpu.VMEM((CHUNK, WIDE), F32),
        pltpu.VMEM((NZ, CHUNK, WIDE), F32),
        pltpu.VMEM((NODES // 2, BLK), F32),
        pltpu.VMEM((nx, NODES // 2, BLK), F32),
        pltpu.VMEM((NODES // 2, BLK), F32),
        pltpu.VMEM((nz, NODES // 2, BLK), F32),
        dma((8,)), dma((2, 2)), dma((2, 2)), dma, dma, dma, dma, dma, dma((nz,)),
        dma, dma, dma, dma,
    ]
    node_mean, new_dual = pl.pallas_call(
        kernel,
        out_shape=[jax.ShapeDtypeStruct(flat, F32)] * 2,
        in_specs=[any_spec] * 8,
        out_specs=[vmem, vmem],
        scratch_shapes=scratch,
        compiler_params=pltpu.CompilerParams(
            collective_id=0, has_side_effects=True, vmem_limit_bytes=56 * 2**20
        ),
        name="round",
    )(
        cost_lin.reshape(flat), na_dual.reshape(flat), prior_mean.reshape(flat),
        kkt_inverse.reshape(SPANS, K, K), tie_coef, res_count, line_class, node_of,
    )
    return node_mean.reshape(cost_lin.shape), new_dual.reshape(cost_lin.shape)


def solution(mesh):
    placed = (
        P("scen", "area", None, None),
        P("scen", "area", None, None),
        P("scen", "area", None, None),
        P("area", None, None, None),
        P("area", None),
        P("area"),
        P("area", None),
        P(None, "scen"),
    )
    return jax.shard_map(
        on_device,
        mesh=mesh,
        in_specs=placed,
        out_specs=(P("scen", "area", None, None), P("scen", "area", None, None)),
        check_vma=False,
    )
```

time: 282 us -> 46.2 us (0.16)
  the two profiles are of different devices: /device:TPU:8 before, /device:TPU:24 now
where the time goes in v1:
time: 46.2 us; the launch traced here: 45.8 us
  Pallas kernels  40.1 us (87%)
  local copies, waits for them, and re-layouts  4.36 us (9%)
  between operations  1.29 us (3%)
    pallas_call x1, Pallas kernels, on_device(): pl.pallas_call(kernel, out_shape=[jax.ShapeDtypeStruct(flat, F32)] * 2, i...  40.1 us
    unnamed x2, local copies, waits for them, and re-layouts  4.36 us

profile of v1, /device:TPU:24, one launch (start us, length us, event | category | flops | bytes accessed | tf_op | source)
XLA Modules:
  0.0 45.8 jit_solution(9078350040903141292)
XLA Ops:
  1.3 40.1 %round.1 = (f32[1008,128]{1,0:T(8,128)}, f32[1008,128]{1,0:T(8,128)}) custom-call(f32[1008,128]{1,0:T(8,128)} %bitcast.7, f32[1008,128]{1,0:T(8,128)} %bitcast.8, f32[1008,128]{1,0:T(8,128)} %bitcast.9, bf16[7,384,384]{2,1,0:T(8,128)(2,1)} %bitcast.6, f32[1,16]{1,0:T(1,128)} %tie_h.1, s32[1]{0:T(128)S(6)} %copy.16.count_h, s32[1,2]{1,0:T(1,128)} %line_h.1, ...), custom_call_target="tpu_custom_call" | custom-call | tf_op jit(solution)/shard_map/round/pallas_call | solution.py:355
  41.4 2.2 %copy.17 = f32[48,1,7,384]{3,1,2,0:T(1,128)} copy(f32[48,1,7,384]{3,1,2,0:T(1,128)} %bitcast.11) | data formatting | bytes 1032192
  43.6 2.2 %copy.18 = f32[48,1,7,384]{3,1,2,0:T(1,128)} copy(f32[48,1,7,384]{3,1,2,0:T(1,128)} %bitcast.10) | data formatting | bytes 1032192

commit v2 on v1

v2 whole, which is shorter than its diff:
```python
import functools

import jax
import jax.numpy as jnp
from jax import lax
from jax.experimental import pallas as pl
from jax.experimental.pallas import tpu as pltpu
from jax.sharding import PartitionSpec as P

F32 = jnp.float32
BF16 = jnp.bfloat16
MESH = pl.DeviceIdType.MESH

SCEN_L = 48
SPANS = 7
K = 384
RES = 16
BLK = 128
NB = K // BLK
ROWS = SCEN_L * SPANS
STRIDE = SPANS * NB
NX, NZ, NA = 4, 8, 16
NODES = 128
CHUNK = NODES // NZ
WIDE = K + BLK

BASE = (126, 124, 120, 112, 96, 64, 0)

X_OFFS = ((2, 0), (1, 0), (3, 0))
Z_OFFS = tuple((0, d) for d in (4, 3, 5, 2, 6, 1, 7))
XALL_OFFS = X_OFFS + ((0, 0),)
A_OFFS = (2, NA - 2, 1, NA - 1)


def split(value):
    high = value.astype(BF16)
    low = (value - high.astype(F32)).astype(BF16)
    return high, low


def dot(a, b):
    return jnp.dot(a, b, preferred_element_type=F32)


def dot_nt(a, b):
    return lax.dot_general(a, b, (((1,), (1,)), ((), ())), preferred_element_type=F32)


def kernel(
    cost_h, dual_h, prior_h, kkt_h, small_r,
    mean_o, base_o, live_o,
    cost_v, dual_v, prior_v, kkt_v, node_v, sel_v, spread_v, spread_all_v, pick_v, pickt_v,
    anchor_v, swh_v, swl_v, sel_all_v,
    exp_v, low_v, high_v,
    part_v, rz_v, sumz_v, rx_v, total_v, gather_v,
    block_v, ra_v, gmat_v, glow_v, ghigh_v, kgap_v,
    in_sem, es_sem, er_sem, zs_sem, zr_sem, xs_sem, xr_sem, as_sem, ar_sem,
    bs_sem, br_sem, gs_sem, gr_sem,
):
    me = lax.axis_index("scen")
    area = lax.axis_index("area")
    my_x = me // NZ
    my_z = lax.rem(me, NZ)
    up = lax.rem(area + 1, NA)
    down = lax.rem(area + NA - 1, NA)

    def peer_z(off):
        return lax.rem(my_z + off[1], NZ)

    def peer(off):
        return lax.rem(my_x + off[0], NX) * NZ + peer_z(off)

    def area_at(step):
        return lax.rem(area + step, NA)

    def send(src, dst, send_sem, recv_sem, device):
        pltpu.make_async_remote_copy(
            src_ref=src, dst_ref=dst, send_sem=send_sem, recv_sem=recv_sem,
            device_id=device, device_id_type=MESH,
        ).start()

    def wait(ref, sem):
        pltpu.make_async_copy(ref, ref, sem).wait()

    loads = [
        pltpu.make_async_copy(src, dst, in_sem.at[i])
        for i, (src, dst) in enumerate(
            ((prior_h, prior_v), (cost_h, cost_v), (dual_h, dual_v), (kkt_h, kkt_v))
        )
    ]
    for load in loads:
        load.start()

    barrier = pltpu.get_barrier_semaphore()
    for off in Z_OFFS + X_OFFS:
        pl.semaphore_signal(barrier, inc=1, device_id={"scen": peer(off)}, device_id_type=MESH)
    for step in A_OFFS:
        for off in XALL_OFFS:
            pl.semaphore_signal(
                barrier, inc=1, device_id={"scen": peer(off), "area": area_at(step)},
                device_id_type=MESH,
            )

    rows = lax.broadcasted_iota(jnp.int32, (K, BLK), 0)
    lanes = lax.broadcasted_iota(jnp.int32, (K, BLK), 1)
    rows_w = lax.broadcasted_iota(jnp.int32, (BLK, K), 0)
    lanes_w = lax.broadcasted_iota(jnp.int32, (BLK, K), 1)
    for j in range(4):
        sel_v[j] = jnp.where(lanes == 32 * j + (rows >> 4), 1.0, 0.0).astype(BF16)
        spread_v[j] = jnp.where(rows_w == 32 * j + (lanes_w >> 4), 1.0, 0.0).astype(BF16)
    spread_all_v[...] = jnp.where((rows_w & 31) == (lanes_w >> 4), 1.0, 0.0).astype(BF16)

    small = small_r[8:16, :]
    tie = small
    for shift in (16, 32, 64):
        tie = tie + pltpu.roll(tie, shift, 1)
    lane_row = lax.broadcasted_iota(jnp.int32, (1, BLK), 1)
    live = jnp.where((lane_row & 15).astype(F32) < small[2:3, 0:1], 1.0, 0.0)
    live_o[...] = jnp.broadcast_to(live, (8, BLK))
    weight = tie[0:1] * live
    live3 = jnp.concatenate([live] * NB, axis=1)
    weight3 = jnp.concatenate([weight] * NB, axis=1)
    for j in range(4):
        placed = jnp.where(rows_w == 32 * j + (lanes_w >> 4), 1.0, 0.0)
        swh_v[j], swl_v[j] = split(placed * weight3)
    sel_all_v[...] = jnp.where((lanes & 31) == (rows >> 4), 1.0, 0.0).astype(BF16)
    left_weight = jnp.broadcast_to(small[1:2, 0:1], (1, BLK)) / 3.0
    right_weight = jnp.broadcast_to(small[1:2, 1:2], (1, BLK)) / 3.0

    node_v[...] = jnp.zeros((BLK, BLK), F32)
    node_v[0:8, :] = small_r[0:8, :]
    node_t = jnp.transpose(node_v[...])
    node_lane = lax.broadcasted_iota(jnp.int32, (SCEN_L, BLK), 1).astype(F32)
    picks = []
    for c in range(SPANS):
        picks.append(jnp.where(node_lane - BASE[c] == node_t[0:SCEN_L, c : c + 1], 1.0, 0.0))
    picks.append(jnp.zeros((K - ROWS, BLK), F32))
    pick = jnp.concatenate(picks, axis=0)
    pickt_v[...] = jnp.transpose(pick).astype(BF16)
    pick_b = pick[0:ROWS].astype(BF16)
    pick_v[:, 0:BLK] = pick_b
    pick_v[:, BLK:] = pick_b

    def place_of(row):
        place = jnp.where(row < 64, 2, jnp.where(row < 96, 1, 0))
        place = jnp.where(row >= 112, 3, place)
        place = jnp.where(row >= 120, 2, place)
        place = jnp.where(row >= 124, 1, place)
        return jnp.where(row >= 126, 0, place)

    def block(ref, c):
        return jnp.concatenate(
            [ref[pl.ds(c * NB + b, SCEN_L, stride=STRIDE), :] for b in range(NB)], axis=1
        )

    def exports(value_of, sweep):
        groups = [None, None]
        for c in range(SPANS):
            g, j = c // 4, c % 4
            high, low = split(value_of(c) * weight3)
            part = dot(jnp.concatenate([high, low], axis=0), sel_v[j])
            part = part[0:SCEN_L] + part[SCEN_L:]
            groups[g] = part if groups[g] is None else groups[g] + part
        exp_v[sweep] = jnp.concatenate(groups, axis=0)

    def send_exports(sweep):
        send(exp_v.at[sweep], low_v.at[sweep], es_sem.at[sweep, 0], er_sem.at[sweep, 0], {"area": up})
        send(exp_v.at[sweep], high_v.at[sweep], es_sem.at[sweep, 1], er_sem.at[sweep, 1], {"area": down})

    def tie_gap(sweep):
        wait(low_v.at[sweep], er_sem.at[sweep, 0])
        wait(high_v.at[sweep], er_sem.at[sweep, 1])
        own = exp_v[sweep]
        return right_weight * (high_v[sweep] - own) + left_weight * (low_v[sweep] - own)

    def targets(gap):
        high, low = split(gap)
        found = []
        for c in range(SPANS):
            g, j = c // 4, c % 4
            rows_g = slice(g * SCEN_L, (g + 1) * SCEN_L)
            wide = dot(jnp.concatenate([high[rows_g], low[rows_g]], axis=0), spread_v[j])
            coupling = 0.5 * weight3 * (wide[0:SCEN_L] + wide[SCEN_L:])
            found.append((anchor_v[c * SCEN_L : (c + 1) * SCEN_L, :] + coupling).astype(BF16))
        return found

    loads[0].wait()
    exports(lambda c: block(prior_v, c), 0)

    loads[1].wait()
    loads[2].wait()
    for c in range(SPANS):
        anchor_v[c * SCEN_L : (c + 1) * SCEN_L, :] = (
            block(prior_v, c) - block(cost_v, c) - block(dual_v, c)
        )
    loads[3].wait()
    highs, lows = [], []
    for c in range(SPANS):
        high, low = split(anchor_v[c * SCEN_L : (c + 1) * SCEN_L, :])
        both = dot_nt(jnp.concatenate([high, low], axis=0), kkt_v[c])
        high, low = split(both[0:SCEN_L] + both[SCEN_L:])
        highs.append(high)
        lows.append(low)
    pick_t = pickt_v[:, 0:ROWS]
    part = dot(pick_t, jnp.concatenate(highs, axis=0)) + dot(pick_t, jnp.concatenate(lows, axis=0))
    sizes = dot(pick_t, jnp.ones((ROWS, BLK), BF16))
    first_high, first_low = split(exp_v[0])
    gathered = [
        jnp.concatenate(
            [half[c // 4 * SCEN_L : (c // 4 + 1) * SCEN_L] for c in range(SPANS)], axis=0
        )
        for half in (first_high, first_low)
    ]
    first_sum = dot(pick_t, gathered[0]) + dot(pick_t, gathered[1])
    place = place_of(lax.broadcasted_iota(jnp.int32, (NODES, BLK), 0))
    group = lax.broadcasted_iota(jnp.int32, (NODES, BLK), 1) >> 5
    extra = jnp.where(group == place, first_sum, 0.0) + jnp.where(
        group == ((place + 2) & 3), sizes, 0.0
    )
    for i in range(NZ):
        rows_i = slice(i * CHUNK, (i + 1) * CHUNK)
        part_v[i, :, 0:K] = part[rows_i]
        part_v[i, :, K:] = extra[rows_i]

    pl.semaphore_wait(barrier, len(Z_OFFS) + len(X_OFFS) + len(A_OFFS) * len(XALL_OFFS))
    send_exports(0)
    for n, off in enumerate(Z_OFFS):
        send(part_v.at[peer_z(off)], rz_v.at[n], zs_sem, zr_sem, {"scen": peer(off)})

    section = jnp.where(my_z < 4, 6, jnp.where(my_z < 6, 5, jnp.where(my_z < 7, 4, 3)))
    slot = jnp.where(my_z < 7, section - 4, 3)

    def echo(c, j):
        wide = dot_nt(kkt_v[c], swh_v[j]) + dot_nt(kkt_v[c], swl_v[j])
        high, low = split(wide)
        return 0.5 * (dot(swh_v[j], high) + dot(swh_v[j], low) + dot(swl_v[j], high))

    gmat_v[0:BLK, :] = echo(section, slot)

    @pl.when(my_z == NZ - 1)
    def _():
        gmat_v[0:BLK, :] += echo(2, 2) + echo(1, 1) + echo(0, 0)

    gmat_v[BLK : BLK + 8, :] = jnp.broadcast_to(left_weight, (8, BLK))
    gmat_v[BLK + 8 :, :] = jnp.broadcast_to(right_weight, (8, BLK))
    send(gmat_v, glow_v, gs_sem.at[0], gr_sem.at[0], {"area": up})
    send(gmat_v, ghigh_v, gs_sem.at[1], gr_sem.at[1], {"area": down})

    first = targets(tie_gap(0))
    exports(lambda c: dot_nt(first[c], kkt_v[c]), 1)
    send_exports(1)

    wait(rz_v, zr_sem)
    acc = part_v[my_z]
    for n in range(len(Z_OFFS)):
        acc = acc + rz_v[n]
    row_c = lax.broadcasted_iota(jnp.int32, (CHUNK, BLK), 0)
    place_c = place_of(row_c + my_z * CHUNK)
    group_c = lax.broadcasted_iota(jnp.int32, (CHUNK, BLK), 1) >> 5
    mine = group_c == place_c
    high, low = split(acc[:, 0:K] * weight3)
    solved = dot(jnp.concatenate([high, low], axis=0), sel_all_v[...])
    solved = jnp.where(mine, solved[0:CHUNK] + solved[CHUNK:], 0.0)
    packed = acc[:, K:] + pltpu.roll(solved, 32, 1)
    block_v[...] = packed
    sumz_v[:, 0:K] = acc[:, 0:K]
    sumz_v[:, K:] = packed
    for k, step in enumerate(A_OFFS):
        for n, off in enumerate(XALL_OFFS):
            send(
                block_v, ra_v.at[k, n], bs_sem, br_sem,
                {"scen": peer(off), "area": area_at(step)},
            )
    for n, off in enumerate(X_OFFS):
        send(sumz_v, rx_v.at[n], xs_sem, xr_sem, {"scen": peer(off)})

    gap = tie_gap(1)
    second = targets(gap)
    for c in range(SPANS):
        current = dot_nt(second[c], kkt_v[c]) * live3
        base = block(dual_v, c) + current
        for b in range(NB):
            base_o[pl.ds(c * NB + b, SCEN_L, stride=STRIDE), :] = base[:, b * BLK : (b + 1) * BLK]

    wait(rx_v, xr_sem)
    wait(ra_v, br_sem)
    wait(glow_v, gr_sem.at[0])
    wait(ghigh_v, gr_sem.at[1])
    acc = sumz_v[...]
    for n in range(len(X_OFFS)):
        acc = acc + rx_v[n]
    packs = {0: acc[:, K:]}
    for k, step in enumerate((2, -2, 1, -1)):
        packs[-step] = (ra_v[k, 0] + ra_v[k, 1]) + (ra_v[k, 2] + ra_v[k, 3])
    first_of = {d: jnp.where(mine, packs[d], 0.0) for d in packs}

    def second_of(d, mat_v):
        left, right = mat_v[BLK : BLK + 1, :], mat_v[BLK + 8 : BLK + 9, :]
        own = first_of[d]
        high, low = split(right * (first_of[d + 1] - own) + left * (first_of[d - 1] - own))
        mat_high, mat_low = split(mat_v[0:BLK, :])
        back = dot_nt(jnp.concatenate([high, low], axis=0), mat_high)
        back = back[0:CHUNK] + back[CHUNK:] + dot_nt(high, mat_low)
        return jnp.where(mine, pltpu.roll(packs[d], BLK - 32, 1) + back, 0.0)

    own = second_of(0, gmat_v)
    gap_sum = right_weight * (second_of(1, ghigh_v) - own) + left_weight * (
        second_of(-1, glow_v) - own
    )
    high, low = split(gap_sum)
    wide = dot(jnp.concatenate([high, low], axis=0), spread_all_v[...])
    high, low = split(0.5 * weight3 * (wide[0:CHUNK] + wide[CHUNK:]))
    both_halves = jnp.concatenate([high, low], axis=0)
    row_k = lax.broadcasted_iota(jnp.int32, (CHUNK, K), 0)

    def solve(c):
        both = dot_nt(both_halves, kkt_v[c])
        return both[0:CHUNK] + both[CHUNK:]

    kgap_v[...] = solve(section)

    @pl.when(my_z == NZ - 1)
    def _():
        found = kgap_v[...]
        for c in (2, 1, 0):
            found = jnp.where(row_k >= BASE[c] - BASE[3], solve(c), found)
        kgap_v[...] = found

    sizes = jnp.max(jnp.where(group_c == ((place_c + 2) & 3), acc[:, K:], 1.0), axis=1, keepdims=True)
    total = (acc[:, 0:K] + kgap_v[...]) / sizes
    total_v[...] = total
    for n, off in enumerate(Z_OFFS):
        send(total_v, gather_v.at[my_z], as_sem, ar_sem.at[n], {"scen": peer(off)})
    gather_v[my_z] = total

    for n, off in enumerate(Z_OFFS):
        source = lax.rem(my_z + NZ - off[1], NZ)
        wait(gather_v.at[source], ar_sem.at[n])
    highs, lows = [], []
    for i in range(NZ):
        high, low = split(gather_v[i])
        highs.append(high)
        lows.append(low)
    averages = jnp.concatenate(highs + lows, axis=0)
    for c in range(SPANS):
        rows_c = slice(c * SCEN_L, (c + 1) * SCEN_L)
        node_mean = dot(pick_v[rows_c, :], averages)
        for b in range(NB):
            place_b = pl.ds(c * NB + b, SCEN_L, stride=STRIDE)
            mean_o[place_b, :] = node_mean[:, b * BLK : (b + 1) * BLK]

    for sweep in range(2):
        wait(exp_v.at[sweep], es_sem.at[sweep, 0])
        wait(exp_v.at[sweep], es_sem.at[sweep, 1])
    wait(rz_v, zs_sem)
    wait(rx_v, xs_sem)
    wait(gather_v.at[0 : NZ - 1], as_sem)
    wait(ra_v, bs_sem)
    wait(gmat_v, gs_sem.at[0])
    wait(gmat_v, gs_sem.at[1])


def on_device(cost_lin, na_dual, prior_mean, kkt_inverse, tie_coef, res_count, line_class, node_of):
    flat = (SCEN_L * STRIDE, BLK)
    hbm = pl.BlockSpec(memory_space=pltpu.HBM)
    vmem = pl.BlockSpec(memory_space=pltpu.VMEM)
    dma = pltpu.SemaphoreType.DMA
    nz, nx = NZ - 1, NX - 1
    scratch = [
        pltpu.VMEM(flat, F32),
        pltpu.VMEM(flat, F32),
        pltpu.VMEM(flat, F32),
        pltpu.VMEM((SPANS, K, K), BF16),
        pltpu.VMEM((BLK, BLK), F32),
        pltpu.VMEM((4, K, BLK), BF16),
        pltpu.VMEM((4, BLK, K), BF16),
        pltpu.VMEM((BLK, K), BF16),
        pltpu.VMEM((ROWS, 2 * BLK), BF16),
        pltpu.VMEM((BLK, K), BF16),
        pltpu.VMEM((ROWS, K), F32),
        pltpu.VMEM((4, BLK, K), BF16),
        pltpu.VMEM((4, BLK, K), BF16),
        pltpu.VMEM((K, BLK), BF16),
        pltpu.VMEM((2, 2 * SCEN_L, BLK), F32),
        pltpu.VMEM((2, 2 * SCEN_L, BLK), F32),
        pltpu.VMEM((2, 2 * SCEN_L, BLK), F32),
        pltpu.VMEM((NZ, CHUNK, WIDE), F32),
        pltpu.VMEM((nz, CHUNK, WIDE), F32),
        pltpu.VMEM((CHUNK, WIDE), F32),
        pltpu.VMEM((nx, CHUNK, WIDE), F32),
        pltpu.VMEM((CHUNK, K), F32),
        pltpu.VMEM((NZ, CHUNK, K), F32),
        pltpu.VMEM((CHUNK, BLK), F32),
        pltpu.VMEM((4, NX, CHUNK, BLK), F32),
        pltpu.VMEM((BLK + 16, BLK), F32),
        pltpu.VMEM((BLK + 16, BLK), F32),
        pltpu.VMEM((BLK + 16, BLK), F32),
        pltpu.VMEM((CHUNK, K), F32),
        dma((4,)), dma((2, 2)), dma((2, 2)), dma, dma, dma, dma, dma, dma((nz,)),
        dma, dma, dma((2,)), dma((2,)),
    ]

    def padded(rows, top):
        return jnp.pad(rows, ((top, 16 - top - rows.shape[0]), (0, BLK - rows.shape[1])))

    small = padded(node_of, 0) + padded(line_class, 9) + padded(res_count.reshape(1, 1), 10)
    small = small.astype(F32) + padded(tie_coef, 8)
    node_mean, base, live = pl.pallas_call(
        kernel,
        out_shape=[jax.ShapeDtypeStruct(flat, F32)] * 2 + [jax.ShapeDtypeStruct((8, BLK), F32)],
        in_specs=[hbm] * 4 + [vmem],
        out_specs=[vmem] * 3,
        scratch_shapes=scratch,
        compiler_params=pltpu.CompilerParams(
            collective_id=0, has_side_effects=True, vmem_limit_bytes=105 * 2**19
        ),
        name="round",
    )(
        cost_lin.reshape(flat), na_dual.reshape(flat), prior_mean.reshape(flat),
        kkt_inverse.reshape(SPANS, K, K), small,
    )
    node_mean = node_mean * live[0:1]
    new_dual = base - node_mean
    return node_mean.reshape(cost_lin.shape), new_dual.reshape(cost_lin.shape)


def solution(mesh):
    placed = (
        P("scen", "area", None, None),
        P("scen", "area", None, None),
        P("scen", "area", None, None),
        P("area", None, None, None),
        P("area", None),
        P("area"),
        P("area", None),
        P(None, "scen"),
    )
    return jax.shard_map(
        on_device,
        mesh=mesh,
        in_specs=placed,
        out_specs=(P("scen", "area", None, None), P("scen", "area", None, None)),
        check_vma=False,
    )
```

time: 46.2 us -> 36.9 us (0.80)
  Pallas kernels: 40.1 us -> 33.7 us
  local copies, waits for them, and re-layouts: 4.36 us -> 0.01 us
  other arithmetic: 0 us -> 1.76 us
    pallas_call x1, Pallas kernels: 40.1 us -> 33.7 us  [on_device(): pl.pallas_call(kernel, out_shape=[jax.ShapeDtypeStruct(flat, F32)] * 2 +...]
    unnamed x2 -> x0, local copies, waits for them, and re-layouts: 4.36 us -> none
    sub x0 -> x1, other arithmetic: none -> 1.03 us  [on_device(): new_dual = base - node_mean]
    add x0 -> x1, other arithmetic: none -> 0.73 us  [on_device(): small = small.astype(F32) + padded(tie_coef, 8)]
where the time goes in v2:
time: 36.9 us; the launch traced here: 36.8 us
  Pallas kernels  33.7 us (91%)
  other arithmetic  1.76 us (5%)
  between operations  1.29 us (3%)
    pallas_call x1, Pallas kernels, on_device(): pl.pallas_call(kernel, out_shape=[jax.ShapeDtypeStruct(flat, F32)] * 2 +...  33.7 us
    sub x1, other arithmetic, on_device(): new_dual = base - node_mean  1.03 us

profile of v2, /device:TPU:24, one launch (start us, length us, event | category | flops | bytes accessed | tf_op | source)
XLA Modules:
  0.0 36.8 jit_solution(9041851441336752998)
XLA Ops:
  1.3 0.7 %pad_add_fusion.small_r = f32[16,128]{1,0:T(8,128)S(1)} fusion(f32[1,16]{1,0:T(1,128)} %param.12, s32[1,1]{1,0:T(1,128)} %bitcast.9, s32[1,2]{1,0:T(1,128)} %param.14, s32[7,48]{1,0:T(8,128)} %param.15), kind=kLoop, calls=%fused_computation.1 | loop fusion | flops 8192 | bytes 9612 | tf_op jit(solution)/shard_map/add | solution.py:407
  2.0 33.7 %round.1 = (f32[1008,128]{1,0:T(8,128)S(1)}, f32[1008,128]{1,0:T(8,128)S(1)}, f32[8,128]{1,0:T(8,128)S(1)}) custom-call(f32[1008,128]{1,0:T(8,128)} %bitcast.11, f32[1008,128]{1,0:T(8,128)} %bitcast.12, f32[1008,128]{1,0:T(8,128)} %bitcast.13, bf16[7,384,384]{2,1,0:T(8,128)(2,1)} %bitcast.10, f32[16,128]{1,0:T(8,128)S(1)} %pad_add_fusion.small_r), custom_call_target="tpu_custom_call" | custom-call | tf_op jit(solution)/shard_map/round/pallas_call | solution.py:408
  35.7 1.0 %fusion = (f32[1008,128]{1,0:T(8,128)}, f32[1008,128]{1,0:T(8,128)}) fusion(f32[1008,128]{1,0:T(8,128)S(1)} %get-tuple-element.7, f32[1008,128]{1,0:T(8,128)S(1)} %get-tuple-element.5, f32[128]{0:T(128)S(1)} %slice_bitcast_fusion), kind=kLoop, calls=%fused_computation.3 | loop fusion | flops 258048 | bytes 2064896 | tf_op jit(solution)/shard_map/sub | solution.py:423
  (1 shorter events, 0.0 us)

commit v3 on v2

--- a/solution.py
+++ b/solution.py
@@ -22,7 +22,7 @@
 NX, NZ, NA = 4, 8, 16
 NODES = 128
 CHUNK = NODES // NZ
-WIDE = K + BLK
+TILE = NB * CHUNK + 8
 
 BASE = (126, 124, 120, 112, 96, 64, 0)
 
@@ -49,11 +49,11 @@
 def kernel(
     cost_h, dual_h, prior_h, kkt_h, small_r,
     mean_o, base_o, live_o,
-    cost_v, dual_v, prior_v, kkt_v, node_v, sel_v, spread_v, spread_all_v, pick_v, pickt_v,
-    anchor_v, swh_v, swl_v, sel_all_v,
+    cost_v, dual_v, prior_v, kkt_v, node_v, sel_v, spread_v, pick_v, pickt_v,
+    anchor_v, swh_v, swl_v, swall_v, sel_all_v, wide_v, wideh_v, widel_v,
     exp_v, low_v, high_v,
     part_v, rz_v, sumz_v, rx_v, total_v, gather_v,
-    block_v, ra_v, gmat_v, glow_v, ghigh_v, kgap_v,
+    ra_v, gmat_v, glow_v, ghigh_v,
     in_sem, es_sem, er_sem, zs_sem, zr_sem, xs_sem, xr_sem, as_sem, ar_sem,
     bs_sem, br_sem, gs_sem, gr_sem,
 ):
@@ -108,7 +108,6 @@
     for j in range(4):
         sel_v[j] = jnp.where(lanes == 32 * j + (rows >> 4), 1.0, 0.0).astype(BF16)
         spread_v[j] = jnp.where(rows_w == 32 * j + (lanes_w >> 4), 1.0, 0.0).astype(BF16)
-    spread_all_v[...] = jnp.where((rows_w & 31) == (lanes_w >> 4), 1.0, 0.0).astype(BF16)
 
     small = small_r[8:16, :]
     tie = small
@@ -123,6 +122,7 @@
     for j in range(4):
         placed = jnp.where(rows_w == 32 * j + (lanes_w >> 4), 1.0, 0.0)
         swh_v[j], swl_v[j] = split(placed * weight3)
+    swall_v[0], swall_v[1] = split(jnp.where((rows_w & 31) == (lanes_w >> 4), 1.0, 0.0) * weight3)
     sel_all_v[...] = jnp.where((lanes & 31) == (rows >> 4), 1.0, 0.0).astype(BF16)
     left_weight = jnp.broadcast_to(small[1:2, 0:1], (1, BLK)) / 3.0
     right_weight = jnp.broadcast_to(small[1:2, 1:2], (1, BLK)) / 3.0
@@ -214,13 +214,25 @@
     first_sum = dot(pick_t, gathered[0]) + dot(pick_t, gathered[1])
     place = place_of(lax.broadcasted_iota(jnp.int32, (NODES, BLK), 0))
     group = lax.broadcasted_iota(jnp.int32, (NODES, BLK), 1) >> 5
-    extra = jnp.where(group == place, first_sum, 0.0) + jnp.where(
-        group == ((place + 2) & 3), sizes, 0.0
-    )
+    high, low = split(part * weight3)
+    solved = dot(jnp.concatenate([high, low], axis=0), sel_all_v[...])
+    solved = solved[0:NODES] + solved[NODES:]
+    in_row = jnp.where(group == place, first_sum, 0.0)
+    in_row = in_row + pltpu.roll(in_row, 32, 1)
+    in_row = in_row + pltpu.roll(in_row, 64, 1)
+    lane_n = lax.broadcasted_iota(jnp.int32, (NODES, BLK), 1) & 31
+    in_row = jnp.where(lane_n >= 24, sizes, in_row)
+    group_8 = lax.broadcasted_iota(jnp.int32, (8, BLK), 1) >> 5
     for i in range(NZ):
-        rows_i = slice(i * CHUNK, (i + 1) * CHUNK)
-        part_v[i, :, 0:K] = part[rows_i]
-        part_v[i, :, K:] = extra[rows_i]
+        top = slice(i * CHUNK, i * CHUNK + 8)
+        low_half = slice(i * CHUNK + 8, (i + 1) * CHUNK)
+        for b in range(NB):
+            part_v[i, b * CHUNK : (b + 1) * CHUNK, :] = part[
+                i * CHUNK : (i + 1) * CHUNK, b * BLK : (b + 1) * BLK
+            ]
+        packed = jnp.where(group_8 == 0, in_row[top], solved[top])
+        packed = jnp.where(group_8 == 2, in_row[low_half], packed)
+        part_v[i, NB * CHUNK :, :] = jnp.where(group_8 == 3, solved[low_half], packed)
 
     pl.semaphore_wait(barrier, len(Z_OFFS) + len(X_OFFS) + len(A_OFFS) * len(XALL_OFFS))
     send_exports(0)
@@ -230,25 +242,26 @@
     section = jnp.where(my_z < 4, 6, jnp.where(my_z < 6, 5, jnp.where(my_z < 7, 4, 3)))
     slot = jnp.where(my_z < 7, section - 4, 3)
 
-    def echo(c, j):
-        wide = dot_nt(kkt_v[c], swh_v[j]) + dot_nt(kkt_v[c], swl_v[j])
-        high, low = split(wide)
-        return 0.5 * (dot(swh_v[j], high) + dot(swh_v[j], low) + dot(swl_v[j], high))
-
-    gmat_v[0:BLK, :] = echo(section, slot)
+    def response(c, j):
+        return dot_nt(kkt_v[c], swh_v[j]) + dot_nt(kkt_v[c], swl_v[j])
+
+    wide_v[...] = response(section, slot)
 
     @pl.when(my_z == NZ - 1)
     def _():
-        gmat_v[0:BLK, :] += echo(2, 2) + echo(1, 1) + echo(0, 0)
-
+        wide_v[...] += response(2, 2) + response(1, 1) + response(0, 0)
+
+    high, low = split(0.5 * wide_v[...])
+    wideh_v[...] = high
+    widel_v[...] = low
+    back = dot(swall_v[0], high) + dot(swall_v[0], low) + dot(swall_v[1], high)
+    row_g = lax.broadcasted_iota(jnp.int32, (BLK, BLK), 0) >> 5
+    lane_g = lax.broadcasted_iota(jnp.int32, (BLK, BLK), 1) >> 5
+    gmat_v[0:BLK, :] = jnp.where(row_g == lane_g, back, 0.0)
     gmat_v[BLK : BLK + 8, :] = jnp.broadcast_to(left_weight, (8, BLK))
     gmat_v[BLK + 8 :, :] = jnp.broadcast_to(right_weight, (8, BLK))
     send(gmat_v, glow_v, gs_sem.at[0], gr_sem.at[0], {"area": up})
     send(gmat_v, ghigh_v, gs_sem.at[1], gr_sem.at[1], {"area": down})
-
-    first = targets(tie_gap(0))
-    exports(lambda c: dot_nt(first[c], kkt_v[c]), 1)
-    send_exports(1)
 
     wait(rz_v, zr_sem)
     acc = part_v[my_z]
@@ -258,21 +271,74 @@
     place_c = place_of(row_c + my_z * CHUNK)
     group_c = lax.broadcasted_iota(jnp.int32, (CHUNK, BLK), 1) >> 5
     mine = group_c == place_c
-    high, low = split(acc[:, 0:K] * weight3)
-    solved = dot(jnp.concatenate([high, low], axis=0), sel_all_v[...])
-    solved = jnp.where(mine, solved[0:CHUNK] + solved[CHUNK:], 0.0)
-    packed = acc[:, K:] + pltpu.roll(solved, 32, 1)
-    block_v[...] = packed
-    sumz_v[:, 0:K] = acc[:, 0:K]
-    sumz_v[:, K:] = packed
+    sumz_v[...] = acc
+    for n, off in enumerate(X_OFFS):
+        send(sumz_v, rx_v.at[n], xs_sem, xr_sem, {"scen": peer(off)})
     for k, step in enumerate(A_OFFS):
         for n, off in enumerate(XALL_OFFS):
             send(
-                block_v, ra_v.at[k, n], bs_sem, br_sem,
+                sumz_v.at[NB * CHUNK :], ra_v.at[k, n], bs_sem, br_sem,
                 {"scen": peer(off), "area": area_at(step)},
             )
-    for n, off in enumerate(X_OFFS):
-        send(sumz_v, rx_v.at[n], xs_sem, xr_sem, {"scen": peer(off)})
+
+    first = targets(tie_gap(0))
+    exports(lambda c: dot_nt(first[c], kkt_v[c]), 1)
+    send_exports(1)
+
+    wait(glow_v, gr_sem.at[0])
+    wait(ghigh_v, gr_sem.at[1])
+    mats = jnp.concatenate([ghigh_v[0:BLK, :], glow_v[0:BLK, :], gmat_v[0:BLK, :]], axis=1)
+    mats_high, mats_low = split(mats)
+    wait(rx_v, xr_sem)
+    wait(ra_v, br_sem)
+    acc = sumz_v[...]
+    for n in range(len(X_OFFS)):
+        acc = acc + rx_v[n]
+    solved = jnp.concatenate([acc[b * CHUNK : (b + 1) * CHUNK] for b in range(NB)], axis=1)
+    packs = {0: acc[NB * CHUNK :]}
+    for k, step in enumerate((2, -2, 1, -1)):
+        packs[-step] = (ra_v[k, 0] + ra_v[k, 1]) + (ra_v[k, 2] + ra_v[k, 3])
+
+    def unpack(packed, first):
+        halves = []
+        for g in (first, first + 2):
+            value = jnp.where(group_8 == g, packed, 0.0)
+            value = value + pltpu.roll(value, 32, 1)
+            halves.append(value + pltpu.roll(value, 64, 1))
+        return jnp.concatenate(halves, axis=0)
+
+    own = unpack(packs[0], 0)
+
+    def first_gap(d, mat_v):
+        left, right = mat_v[BLK : BLK + 1, :], mat_v[BLK + 8 : BLK + 9, :]
+        gap_d = right * (packs[d + 1] - packs[d]) + left * (packs[d - 1] - packs[d])
+        return jnp.where(mine, unpack(gap_d, 0), 0.0)
+
+    both_weights = left_weight + right_weight
+    gaps = jnp.concatenate(
+        [
+            right_weight * first_gap(1, ghigh_v),
+            left_weight * first_gap(-1, glow_v),
+            -both_weights * first_gap(0, gmat_v),
+        ],
+        axis=1,
+    )
+    high, low = split(gaps)
+    back = dot_nt(jnp.concatenate([high, low], axis=0), mats_high)
+    back = back[0:CHUNK] + back[CHUNK:] + dot_nt(high, mats_low)
+    anchor_gap = right_weight * (packs[1] - packs[0]) + left_weight * (packs[-1] - packs[0])
+    gap_sum = jnp.where(mine, unpack(anchor_gap, 1) + back, 0.0)
+    high, low = split(gap_sum)
+    kgap = dot_nt(jnp.concatenate([high, low], axis=0), wideh_v[...])
+    kgap = kgap[0:CHUNK] + kgap[CHUNK:] + dot_nt(high, widel_v[...])
+
+    lane_c = lax.broadcasted_iota(jnp.int32, (CHUNK, BLK), 1) & 31
+    sizes = jnp.max(jnp.where(lane_c >= 24, own, 1.0), axis=1, keepdims=True)
+    total = (solved + kgap) / sizes
+    total_v[...] = total
+    for n, off in enumerate(Z_OFFS):
+        send(total_v, gather_v.at[my_z], as_sem, ar_sem.at[n], {"scen": peer(off)})
+    gather_v[my_z] = total
 
     gap = tie_gap(1)
     second = targets(gap)
@@ -281,57 +347,6 @@
         base = block(dual_v, c) + current
         for b in range(NB):
             base_o[pl.ds(c * NB + b, SCEN_L, stride=STRIDE), :] = base[:, b * BLK : (b + 1) * BLK]
-
-    wait(rx_v, xr_sem)
-    wait(ra_v, br_sem)
-    wait(glow_v, gr_sem.at[0])
-    wait(ghigh_v, gr_sem.at[1])
-    acc = sumz_v[...]
-    for n in range(len(X_OFFS)):
-        acc = acc + rx_v[n]
-    packs = {0: acc[:, K:]}
-    for k, step in enumerate((2, -2, 1, -1)):
-        packs[-step] = (ra_v[k, 0] + ra_v[k, 1]) + (ra_v[k, 2] + ra_v[k, 3])
-    first_of = {d: jnp.where(mine, packs[d], 0.0) for d in packs}
-
-    def second_of(d, mat_v):
-        left, right = mat_v[BLK : BLK + 1, :], mat_v[BLK + 8 : BLK + 9, :]
-        own = first_of[d]
-        high, low = split(right * (first_of[d + 1] - own) + left * (first_of[d - 1] - own))
-        mat_high, mat_low = split(mat_v[0:BLK, :])
-        back = dot_nt(jnp.concatenate([high, low], axis=0), mat_high)
-        back = back[0:CHUNK] + back[CHUNK:] + dot_nt(high, mat_low)
-        return jnp.where(mine, pltpu.roll(packs[d], BLK - 32, 1) + back, 0.0)
-
-    own = second_of(0, gmat_v)
-    gap_sum = right_weight * (second_of(1, ghigh_v) - own) + left_weight * (
-        second_of(-1, glow_v) - own
-    )
-    high, low = split(gap_sum)
-    wide = dot(jnp.concatenate([high, low], axis=0), spread_all_v[...])
-    high, low = split(0.5 * weight3 * (wide[0:CHUNK] + wide[CHUNK:]))
-    both_halves = jnp.concatenate([high, low], axis=0)
-    row_k = lax.broadcasted_iota(jnp.int32, (CHUNK, K), 0)
-
-    def solve(c):
-        both = dot_nt(both_halves, kkt_v[c])
-        return both[0:CHUNK] + both[CHUNK:]
-
-    kgap_v[...] = solve(section)
-
-    @pl.when(my_z == NZ - 1)
-    def _():
-        found = kgap_v[...]
-        for c in (2, 1, 0):
-            found = jnp.where(row_k >= BASE[c] - BASE[3], solve(c), found)
-        kgap_v[...] = found
-
-    sizes = jnp.max(jnp.where(group_c == ((place_c + 2) & 3), acc[:, K:], 1.0), axis=1, keepdims=True)
-    total = (acc[:, 0:K] + kgap_v[...]) / sizes
-    total_v[...] = total
-    for n, off in enumerate(Z_OFFS):
-        send(total_v, gather_v.at[my_z], as_sem, ar_sem.at[n], {"scen": peer(off)})
-    gather_v[my_z] = total
 
     for n, off in enumerate(Z_OFFS):
         source = lax.rem(my_z + NZ - off[1], NZ)
@@ -374,28 +389,29 @@
         pltpu.VMEM((BLK, BLK), F32),
         pltpu.VMEM((4, K, BLK), BF16),
         pltpu.VMEM((4, BLK, K), BF16),
-        pltpu.VMEM((BLK, K), BF16),
         pltpu.VMEM((ROWS, 2 * BLK), BF16),
         pltpu.VMEM((BLK, K), BF16),
         pltpu.VMEM((ROWS, K), F32),
         pltpu.VMEM((4, BLK, K), BF16),
         pltpu.VMEM((4, BLK, K), BF16),
+        pltpu.VMEM((2, BLK, K), BF16),
+        pltpu.VMEM((K, BLK), BF16),
+        pltpu.VMEM((K, BLK), F32),
+        pltpu.VMEM((K, BLK), BF16),
         pltpu.VMEM((K, BLK), BF16),
         pltpu.VMEM((2, 2 * SCEN_L, BLK), F32),
         pltpu.VMEM((2, 2 * SCEN_L, BLK), F32),
         pltpu.VMEM((2, 2 * SCEN_L, BLK), F32),
-        pltpu.VMEM((NZ, CHUNK, WIDE), F32),
-        pltpu.VMEM((nz, CHUNK, WIDE), F32),
-        pltpu.VMEM((CHUNK, WIDE), F32),
-        pltpu.VMEM((nx, CHUNK, WIDE), F32),
+        pltpu.VMEM((NZ, TILE, BLK), F32),
+        pltpu.VMEM((nz, TILE, BLK), F32),
+        pltpu.VMEM((TILE, BLK), F32),
+        pltpu.VMEM((nx, TILE, BLK), F32),
         pltpu.VMEM((CHUNK, K), F32),
         pltpu.VMEM((NZ, CHUNK, K), F32),
-        pltpu.VMEM((CHUNK, BLK), F32),
-        pltpu.VMEM((4, NX, CHUNK, BLK), F32),
+        pltpu.VMEM((4, NX, 8, BLK), F32),
         pltpu.VMEM((BLK + 16, BLK), F32),
         pltpu.VMEM((BLK + 16, BLK), F32),
         pltpu.VMEM((BLK + 16, BLK), F32),
-        pltpu.VMEM((CHUNK, K), F32),
         dma((4,)), dma((2, 2)), dma((2, 2)), dma, dma, dma, dma, dma, dma((nz,)),
         dma, dma, dma((2,)), dma((2,)),
     ]

time: 36.9 us -> 36.1 us (0.978)
  Pallas kernels: 33.7 us -> 32.8 us
    pallas_call x1, Pallas kernels: 33.7 us -> 32.8 us  [on_device(): pl.pallas_call(kernel, out_shape=[jax.ShapeDtypeStruct(flat, F32)] * 2 +...]
where the time goes in v3:
time: 36.1 us; the launch traced here: 35.9 us
  Pallas kernels  32.8 us (91%)
  other arithmetic  1.76 us (5%)
  between operations  1.29 us (4%)
    pallas_call x1, Pallas kernels, on_device(): pl.pallas_call(kernel, out_shape=[jax.ShapeDtypeStruct(flat, F32)] * 2 +...  32.8 us
    sub x1, other arithmetic, on_device(): new_dual = base - node_mean  1.03 us
    add x1, other arithmetic, on_device(): small = small.astype(F32) + padded(tie_coef, 8)  0.73 us

profile of v3, /device:TPU:24, one launch (start us, length us, event | category | flops | bytes accessed | tf_op | source)
XLA Modules:
  0.0 35.9 jit_solution(10019672280559973643)
XLA Ops:
  1.3 0.7 %pad_add_fusion.small_r = f32[16,128]{1,0:T(8,128)S(1)} fusion(f32[1,16]{1,0:T(1,128)} %param.12, s32[1,1]{1,0:T(1,128)} %bitcast.9, s32[1,2]{1,0:T(1,128)} %param.14, s32[7,48]{1,0:T(8,128)} %param.15), kind=kLoop, calls=%fused_computation.1 | loop fusion | flops 8192 | bytes 9612 | tf_op jit(solution)/shard_map/add | solution.py:423
  2.0 32.8 %round.1 = (f32[1008,128]{1,0:T(8,128)S(1)}, f32[1008,128]{1,0:T(8,128)S(1)}, f32[8,128]{1,0:T(8,128)S(1)}) custom-call(f32[1008,128]{1,0:T(8,128)} %bitcast.11, f32[1008,128]{1,0:T(8,128)} %bitcast.12, f32[1008,128]{1,0:T(8,128)} %bitcast.13, bf16[7,384,384]{2,1,0:T(8,128)(2,1)} %bitcast.10, f32[16,128]{1,0:T(8,128)S(1)} %pad_add_fusion.small_r), custom_call_target="tpu_custom_call" | custom-call | tf_op jit(solution)/shard_map/round/pallas_call | solution.py:424
  34.9 1.0 %fusion = (f32[1008,128]{1,0:T(8,128)}, f32[1008,128]{1,0:T(8,128)}) fusion(f32[1008,128]{1,0:T(8,128)S(1)} %get-tuple-element.7, f32[1008,128]{1,0:T(8,128)S(1)} %get-tuple-element.5, f32[128]{0:T(128)S(1)} %slice_bitcast_fusion), kind=kLoop, calls=%fused_computation.3 | loop fusion | flops 258048 | bytes 2064896 | tf_op jit(solution)/shard_map/sub | solution.py:439
  (1 shorter events, 0.0 us)

commit v4 on v3

--- a/solution.py
+++ b/solution.py
@@ -272,14 +272,14 @@
     group_c = lax.broadcasted_iota(jnp.int32, (CHUNK, BLK), 1) >> 5
     mine = group_c == place_c
     sumz_v[...] = acc
-    for n, off in enumerate(X_OFFS):
-        send(sumz_v, rx_v.at[n], xs_sem, xr_sem, {"scen": peer(off)})
     for k, step in enumerate(A_OFFS):
         for n, off in enumerate(XALL_OFFS):
             send(
                 sumz_v.at[NB * CHUNK :], ra_v.at[k, n], bs_sem, br_sem,
                 {"scen": peer(off), "area": area_at(step)},
             )
+    for n, off in enumerate(X_OFFS):
+        send(sumz_v, rx_v.at[n], xs_sem, xr_sem, {"scen": peer(off)})
 
     first = targets(tie_gap(0))
     exports(lambda c: dot_nt(first[c], kkt_v[c]), 1)

time: 36.1 us -> 36 us (level)
  no operation moved by 1% of the time
where the time goes in v4:
time: 36 us; the launch traced here: 35.9 us
  Pallas kernels  32.8 us (91%)
  other arithmetic  1.76 us (5%)
  between operations  1.29 us (4%)
    pallas_call x1, Pallas kernels, on_device(): pl.pallas_call(kernel, out_shape=[jax.ShapeDtypeStruct(flat, F32)] * 2 +...  32.8 us
    sub x1, other arithmetic, on_device(): new_dual = base - node_mean  1.03 us
    add x1, other arithmetic, on_device(): small = small.astype(F32) + padded(tie_coef, 8)  0.73 us

profile of v4, /device:TPU:24, one launch (start us, length us, event | category | flops | bytes accessed | tf_op | source)
XLA Modules:
  0.0 35.9 jit_solution(14608478639307311426)
XLA Ops:
  1.3 0.7 %pad_add_fusion.small_r = f32[16,128]{1,0:T(8,128)S(1)} fusion(f32[1,16]{1,0:T(1,128)} %param.12, s32[1,1]{1,0:T(1,128)} %bitcast.9, s32[1,2]{1,0:T(1,128)} %param.14, s32[7,48]{1,0:T(8,128)} %param.15), kind=kLoop, calls=%fused_computation.1 | loop fusion | flops 8192 | bytes 9612 | tf_op jit(solution)/shard_map/add | solution.py:423
  2.0 32.8 %round.1 = (f32[1008,128]{1,0:T(8,128)S(1)}, f32[1008,128]{1,0:T(8,128)S(1)}, f32[8,128]{1,0:T(8,128)S(1)}) custom-call(f32[1008,128]{1,0:T(8,128)} %bitcast.11, f32[1008,128]{1,0:T(8,128)} %bitcast.12, f32[1008,128]{1,0:T(8,128)} %bitcast.13, bf16[7,384,384]{2,1,0:T(8,128)(2,1)} %bitcast.10, f32[16,128]{1,0:T(8,128)S(1)} %pad_add_fusion.small_r), custom_call_target="tpu_custom_call" | custom-call | tf_op jit(solution)/shard_map/round/pallas_call | solution.py:424
  34.8 1.0 %fusion = (f32[1008,128]{1,0:T(8,128)}, f32[1008,128]{1,0:T(8,128)}) fusion(f32[1008,128]{1,0:T(8,128)S(1)} %get-tuple-element.7, f32[1008,128]{1,0:T(8,128)S(1)} %get-tuple-element.5, f32[128]{0:T(128)S(1)} %slice_bitcast_fusion), kind=kLoop, calls=%fused_computation.3 | loop fusion | flops 258048 | bytes 2064896 | tf_op jit(solution)/shard_map/sub | solution.py:439
  (1 shorter events, 0.0 us)
